TPU v7x, 32 devices: a whole 2x2x4 slice. The times are simulated.
32 devices in a mesh: rep: 2 (over x), kv: 4 (over y, core), tp: 4 (over z).
Axes of the slice: x: 2, y: 2, z: 4, core: 2. Of those that a mesh axis runs over, the one named last changes fastest.
Arguments:
- token_state: bfloat16 [32, 1280], P('kv'), may hold values from -6 to 6
- attn_gain: float32 [1280], replicated, may hold values from 0.1 to 1.9
- qkv_weight: bfloat16 [1280, 3840], P(None, 'tp'), may hold values from -0.15625 to 0.15625
- out_weight: bfloat16 [1280, 1280], P('tp'), may hold values from -0.15625 to 0.15625
- mlp_gain: float32 [1280], replicated, may hold values from 0.1 to 1.9
- up_weight: bfloat16 [1280, 1280], P(None, 'tp'), may hold values from -0.15625 to 0.15625
- down_weight: bfloat16 [1280, 1280], P('tp'), may hold values from -0.15625 to 0.15625
- kv_cache: bfloat16 [2, 44, 512, 2560], P('rep', 'kv', None, 'tp'), as said below
- home_replica: int32 [32], replicated, may hold values from 0 to 1, as said below
- moving: int32 [32], replicated, may hold values 0 or 1
- cache_length: int32 [32], replicated, may hold values from 1 to 5632, as said below
- block_owner: int32 [2, 44], P('rep', 'kv'), may hold values from 0 to 32, as said below
- block_index: int32 [2, 44], P('rep', 'kv'), may hold values from 0 to 10, as said below
Outputs:
- hidden_out: float32 [2, 32, 1280], P('rep', 'kv')
- new_entries: float32 [2, 32, 2560], P('rep', 'kv', 'tp')
Inputs may be any that keep to these rules, and one draw needn't show every extreme that they name: `home_replica`: both replicas hold at least one slot. `cache_length`: a slot's cache lies whole in the pool of its home replica; one slot of each replica has exactly 5632 tokens. `block_owner`: a slot owns exactly ceil(cache_length / 512) blocks, all in the pool of its home replica; 32 marks a free block. `block_index`: the blocks of one slot carry 0 to ceil(cache_length / 512) - 1, each once; free blocks carry 0. `kv_cache`: keys may be large in a few tokens.
All inputs are finite; a program needn't handle non-finite values.
Results may differ from a plain program's by a relative error of at most 0.0061.
Values may be sent and summed in bfloat16 or wider, within the bound.
A program may use at most 128 MiB of HBM per device.

v0:
```python
import jax
import jax.numpy as jnp
from jax import lax
from jax.sharding import PartitionSpec as P

HD = 80


very_low = -1e30
norm_eps = 1e-06


def combined_all(value, axis, join):
    pieces = jax.tree.map(lambda part: lax.all_gather(part, axis), value)
    head = jax.tree.map(lambda part: part[0], pieces)
    tail = jax.tree.map(lambda part: part[1:], pieces)
    running, _ = lax.scan(lambda running, share: (join(running, share), None), head, tail)
    return running


def from_partner(block, axis, bit):
    count = lax.axis_size(axis)
    route = []
    for low in range(count):
        high = low | 1 << bit
        if high != low and high < count:
            route += [(low, high), (high, low)]
    return lax.ppermute(block, axis, route)


def root_norm(values_in, gain_vector):
    values_in = values_in.astype(jnp.float32)
    scaled = values_in * lax.rsqrt(
        jnp.mean(values_in * values_in, axis=-1, keepdims=True) + norm_eps
    )
    return scaled * gain_vector


def softmax_merge(earlier, later):
    peak_one, total_one, sums_one = earlier
    peak_two, total_two, sums_two = later
    joint_peak = jnp.maximum(peak_one, peak_two)
    factor_one = jnp.exp(peak_one - joint_peak)
    factor_two = jnp.exp(peak_two - joint_peak)
    return (
        joint_peak,
        total_one * factor_one + total_two * factor_two,
        sums_one * factor_one[..., None] + sums_two * factor_two[..., None],
    )


def body(
    token_state,
    attn_gain,
    qkv_weight,
    out_weight,
    mlp_gain,
    up_weight,
    down_weight,
    kv_cache,
    home_replica,
    moving,
    cache_length,
    block_owner,
    block_index,
):
    rows_kv = token_state.shape[0]
    requests = home_replica.shape[0]
    head_count = out_weight.shape[0] // HD
    normed = root_norm(lax.all_gather(token_state, "kv", axis=0, tiled=True), attn_gain).astype(
        jnp.bfloat16
    )
    projected = jnp.dot(normed, qkv_weight, preferred_element_type=jnp.float32)
    projected = projected.reshape(requests, head_count, 3, HD)
    query = (projected[:, :, 0] * HD ** (-0.5)).astype(jnp.bfloat16)
    fresh_pairs = projected[:, :, 1:].astype(jnp.bfloat16)
    blocks = kv_cache[0].reshape(kv_cache.shape[1], kv_cache.shape[2], head_count, 2, HD)
    owners = block_owner[0]
    is_owned = owners < requests
    clipped = jnp.minimum(owners, requests - 1)
    block_query = query[clipped]
    scores = jnp.einsum(
        "bhd,bthd->bth", block_query, blocks[:, :, :, 0], preferred_element_type=jnp.float32
    )
    positions = (
        block_index[0][:, None] * blocks.shape[1]
        + jnp.arange(blocks.shape[1], dtype=jnp.int32)[None, :]
    )
    usable = is_owned[:, None] & (positions < cache_length[clipped][:, None])
    masked = jnp.where(usable[:, :, None], scores, very_low)
    block_peak = jnp.max(masked, axis=1)
    onehot = (clipped[:, None] == jnp.arange(requests, dtype=jnp.int32)[None, :]) & is_owned[
        :, None
    ]
    local_peak = jnp.max(jnp.where(onehot[:, :, None], block_peak[:, None, :], very_low), axis=0)
    shift_by = local_peak[clipped]
    weights = jnp.where(usable[:, :, None], jnp.exp(masked - shift_by[:, None, :]), 0.0)
    block_total = jnp.sum(weights, axis=1)
    block_acc = jnp.einsum(
        "bth,bthd->bhd",
        weights.astype(jnp.bfloat16),
        blocks[:, :, :, 1],
        preferred_element_type=jnp.float32,
    )
    selector = onehot.astype(jnp.float32)
    local_total = jnp.einsum("bq,bh->qh", selector, block_total, precision=lax.Precision.HIGHEST)
    local_acc = jnp.einsum("bq,bhd->qhd", selector, block_acc, precision=lax.Precision.HIGHEST)
    local_parts = (local_peak, local_total, local_acc)
    replica = lax.axis_index("rep")
    row_start = lax.axis_index("kv") * rows_kv

    def own_rows(source_array):
        return lax.dynamic_slice_in_dim(source_array, row_start, rows_kv, 0)

    global_peak, global_total, global_acc = combined_all(
        (local_parts[0], local_parts[1], local_parts[2]), "kv", softmax_merge
    )
    global_peak = own_rows(global_peak)
    global_total = own_rows(global_total)
    global_acc = own_rows(global_acc)
    pair_rows = own_rows(fresh_pairs)
    query_rows = own_rows(query)
    self_score = jnp.sum(
        query_rows.astype(jnp.float32) * pair_rows[:, :, 0].astype(jnp.float32), axis=-1
    )
    top_score = jnp.maximum(global_peak, self_score)
    cache_scale = jnp.exp(global_peak - top_score)
    self_weight = jnp.exp(self_score - top_score)
    rounded_self = lax.optimization_barrier(self_weight.astype(jnp.bfloat16)).astype(jnp.float32)
    denominator = global_total * cache_scale + self_weight
    numerator = global_acc * cache_scale[..., None] + rounded_self[..., None] * pair_rows[
        :, :, 1
    ].astype(jnp.float32)
    attended = (
        (numerator / denominator[..., None]).astype(jnp.bfloat16).reshape(rows_kv, head_count * HD)
    )
    home_rows = own_rows(home_replica)
    attended_other = from_partner(attended, "rep", 0)
    attended = jnp.where((home_rows == replica)[:, None], attended, attended_other)
    partial_out = jnp.dot(attended, out_weight, preferred_element_type=jnp.float32)
    residual = token_state.astype(jnp.float32) + lax.psum(partial_out, "tp")
    normed_mlp = root_norm(residual, mlp_gain).astype(jnp.bfloat16)
    activated = jax.nn.gelu(
        jnp.dot(normed_mlp, up_weight, preferred_element_type=jnp.float32), approximate=True
    ).astype(jnp.bfloat16)
    result = residual + lax.psum(
        jnp.dot(activated, down_weight, preferred_element_type=jnp.float32), "tp"
    )
    target = jnp.bitwise_xor(home_rows, own_rows(moving))
    served_here = target == replica
    hidden_out = jnp.where(served_here[:, None], result, jnp.zeros_like(result))[None]
    entries = own_rows(projected[:, :, 1:]).reshape(rows_kv, head_count * 2 * HD)
    new_entries = jnp.where(served_here[:, None], entries, jnp.zeros_like(entries))[None]
    return (hidden_out, new_entries)


def solution(mesh):
    return jax.shard_map(
        body,
        mesh=mesh,
        in_specs=(
            P("kv", None),
            P(),
            P(None, "tp"),
            P("tp", None),
            P(),
            P(None, "tp"),
            P("tp", None),
            P("rep", "kv", None, "tp"),
            P(),
            P(),
            P(),
            P("rep", "kv"),
            P("rep", "kv"),
        ),
        out_specs=(P("rep", "kv", None), P("rep", "kv", "tp")),
        check_vma=False,
    )
```

profile of v0, /device:TPU:0, one launch (start us, length us, event | category | flops | bytes accessed | tf_op | source)
XLA Modules:
  0.0 93.2 jit_solution(6905638866931945062)
XLA Ops:
  0.6 0.0 copy-start
  0.6 0.0 copy-start.6
  0.7 0.0 copy-start.1
  0.7 0.8 compare_bitcast_fusion
  1.5 0.7 minimum_bitcast_fusion
  2.1 0.7 fusion.50
  2.8 6.5 %all_gather.21 = bf16[32,1280]{1,0:T(8,128)(2,1)S(1)} all-gather(bf16[8,1280]{1,0:T(8,128)(2,1)} %param.15), channel_id=1, replica_groups=mesh['rep'=2,'kv'=4,'tp'=4] {'kv'}, dimensions={0}, use_global_device_ids=true | all-gather | bytes 102400 | tf_op jit(solution)/shard_map/all_gather | solution.py:70
  9.3 0.1 fusion.6
  9.4 0.0 copy-done
  9.4 1.5 %fusion.12 = f32[32,960]{1,0:T(8,128)S(1)} fusion(bf16[1280,960]{0,1:T(8,128)(2,1)S(1)} %copy-done, bf16[32,1280]{1,0:T(8,128)(2,1)S(1)} %all_gather.21, f32[1280]{0:T(1024)} %param.16, f32[32]{0:T(128)S(1)} %add_rsqrt_fusion.1), kind=kOutput, calls=%fused_computation.29 | convolution fusion | flops 78807040 | bytes 2667648 | tf_op jit(solution)/shard_map/dot_general | solution.py:73
  10.9 0.3 reshape.203
  11.3 0.1 slice.74
  11.4 0.0 copy-done.6
  11.5 0.0 copy-done.1
  11.5 0.7 gather_fusion
  12.1 0.6 gather_fusion.1
  12.7 10.3 %copy.96 = bf16[1,11,512,640]{2,3,1,0:T(8,128)(2,1)} copy(bf16[1,11,512,640]{3,2,1,0:T(8,128)(2,1)} %param.22) | data formatting | bytes 14417920 | tf_op args[7]
  23.0 0.1 fusion.38
  23.1 0.1 fusion.20
  23.2 2.6 %fusion.5 = f32[11,4,1,512]{3,2,1,0:T(1,128)S(1)} fusion(bf16[11,512,4,2,80]{1,4,3,2,0:T(8,128)(2,1)} %bitcast.90, bf16[11,4,80,1]{2,1,0,3:T(4,128)(2,1)S(1)} %bitcast.93), kind=kOutput, calls=%fused_computation.16 | convolution fusion | flops 3604480 | bytes 3701632 | tf_op jit(solution)/shard_map/bhd,bthd->bth/dot_general | solution.py:82
  25.8 0.1 bitcast_reduce_fusion
  25.9 0.1 select_reduce_fusion
  26.0 5.4 %all-gather.3 = f32[4,32,4]{1,2,0:T(4,128)S(1)} all-gather(f32[1,32,4]{1,2,0:T(4,128)S(1)} %bitcast.94), channel_id=2, replica_groups=mesh['rep'=2,'kv'=4,'tp'=4] {'kv'}, dimensions={0}, use_global_device_ids=true | all-gather | bytes 2560 | tf_op jit(solution)/shard_map/all_gather | solution.py:14
  31.4 0.1 copy.97
  31.5 0.6 gather_fusion.2
  32.1 0.2 convert_bitcast_fusion
  32.3 0.2 convolution_bitcast_fusion
  32.5 5.2 %all-gather.4 = f32[4,32,4]{1,2,0:T(4,128)S(1)} all-gather(f32[1,32,4]{1,2,0:T(4,128)S(1)} %convolution_bitcast_fusion), channel_id=3, replica_groups=mesh['rep'=2,'kv'=4,'tp'=4] {'kv'}, dimensions={0}, use_global_device_ids=true | all-gather | bytes 2560 | tf_op jit(solution)/shard_map/all_gather | solution.py:14
  37.6 0.0 copy-start.3
  37.7 3.1 %fusion.4 = f32[11,4,1,80]{3,2,1,0:T(1,128)S(1)} fusion(bf16[11,512,4,2,80]{1,4,3,2,0:T(8,128)(2,1)} %bitcast.91, bf16[11,512,4,1]{1,2,0,3:T(4,128)(2,1)S(1)} %get-tuple-element.120), kind=kOutput, calls=%fused_computation.14 | convolution fusion | flops 3604480 | bytes 3663616 | tf_op jit(solution)/shard_map/bth,bthd->bhd/dot_general | solution.py:99
  40.7 0.3 fusion.17
  41.1 6.0 %all-gather.2 = f32[128,4,80]{2,0,1:T(8,128)S(1)} all-gather(f32[32,4,80]{2,0,1:T(8,128)S(1)} %fusion.17), channel_id=4, replica_groups=mesh['rep'=2,'kv'=4,'tp'=4] {'kv'}, dimensions={0}, use_global_device_ids=true | all-gather | bytes 204800 | tf_op jit(solution)/shard_map/all_gather | solution.py:14
  47.1 0.1 multiply_reduce_fusion.1
  47.2 0.1 copy.115
  47.3 1.4 %while.14 = (s32[]{:T(128)}, f32[32,4]{0,1:T(4,128)S(1)}, f32[32,4]{0,1:T(4,128)S(1)}, f32[32,4,80]{2,1,0:T(4,128)S(1)}, f32[3,32,4]{1,2,0:T(4,128)S(1)}, /*inde...) while((s32[]{:T(128)}, f32[32,4]{0,1:T(4,128)S(1)}, f32[32,4]{0,1:T(4,128)S(1)}, ...), condition=%wide.region_5.6_spmd, body=%wide.region_4.5_spmd.sunk | while | flops 31490 | bytes 212069 | solution.py:17
  47.4 0.1 copy.153
  47.5 0.1 copy.154
  47.5 0.2 fusion.68
  47.8 0.1 copy.153
  47.9 0.1 copy.154
  48.0 0.2 fusion.68
  48.3 0.1 copy.153
  48.4 0.1 copy.154
  48.5 0.2 fusion.68
  48.7 0.1 copy.101
  48.8 0.1 copy.106
  48.9 0.1 copy.107
  49.0 0.1 copy.104
  49.1 0.1 copy.105
  49.1 0.1 fusion.28
  49.3 0.1 reshape.204
  49.3 1.5 %collective-permute-start = (bf16[8,320]{1,0:T(8,128)(2,1)S(1)}, bf16[8,320]{1,0:T(8,128)(2,1)S(1)}, u32[]{:S(2)}, u32[]{:S(2)}) collective-permute-start(bf16[8,320]{1,0:T(8,128)(2,1)S(1)} %reshape.204), channel_id=1, source_target_pairs={{0,16},{16,0},{1,17},{17,1},{2,18},{18,2},{3,19},{19,3},{4,20},{20... | collective-permute-start | bytes 15368 | tf_op jit(solution)/shard_map/ppermute | solution.py:28
  50.9 0.1 reshape.205
  51.0 0.0 copy-done.4
  51.0 0.1 xor_compare_fusion
  51.1 0.7 broadcast_select_fusion
  51.8 1.2 %collective-permute-done = bf16[8,320]{1,0:T(8,128)(2,1)S(1)} collective-permute-done((bf16[8,320]{1,0:T(8,128)(2,1)S(1)}, bf16[8,320]{1,0:T(8,128)(2,1)S(1)}, u32[]{:S(2)}, u32[]{:S(2)}) %collective-permute-start) | collective-permute-done | bytes 5152 | tf_op jit(solution)/shard_map/ppermute | solution.py:28
  53.0 1.4 %fusion.44 = f32[8,1280]{1,0:T(8,128)S(1)} fusion(bf16[320,1280]{1,0:T(8,128)(2,1)} %param.18, bf16[8,320]{1,0:T(8,128)(2,1)S(1)} %reshape.204, bf16[8,320]{1,0:T(8,128)(2,1)S(1)} %collective-permute-done, pred[8]{0:T(512)(128)(4,1)S(1)} %get-tuple-element.124), kind=kOutput, calls=%fused_computation.74 | convolution fusion | flops 6556160 | bytes 870408 | tf_op jit(solution)/shard_map/dot_general | solution.py:140
  54.4 19.7 %psum.14 = f32[8,1280]{1,0:T(8,128)S(1)} all-reduce(f32[8,1280]{1,0:T(8,128)S(1)} %fusion.44), channel_id=1, replica_groups=mesh['rep'=2,'kv'=4,'tp'=4] {'tp'}, use_global_device_ids=true, to_apply=%region_7.8 | all-reduce | flops 10240 | bytes 81920 | tf_op jit(solution)/shard_map/psum | solution.py:141
  74.1 0.1 multiply_reduce_fusion
  74.2 0.0 copy-done.3
  74.2 2.1 %fusion.37 = f32[8,1280]{1,0:T(8,128)S(1)} fusion(bf16[320,1280]{1,0:T(8,128)(2,1)} %param.21, bf16[1280,320]{0,1:T(8,128)(2,1)} %param.20, f32[1280]{0:T(1024)S(1)} %copy-done.3, f32[8]{0:T(128)S(1)} %add_rsqrt_fusion, f32[8,1280]{1,0:T(8,128)S(1)} %psum.14, bf16[8,1280]{1,0:T(8,128)(2,1)S(1)} %copy-done.2), kind=kOutput, calls=%fused_computation.64 | convolution fusion | flops 13181440 | bytes 1745952 | tf_op jit(solution)/shard_map/dot_general | solution.py:147
  76.4 16.1 %psum.15 = f32[8,1280]{1,0:T(8,128)S(1)} all-reduce(f32[8,1280]{1,0:T(8,128)S(1)} %fusion.37), channel_id=1, replica_groups=mesh['rep'=2,'kv'=4,'tp'=4] {'tp'}, use_global_device_ids=true, to_apply=%region_9.10 | all-reduce | flops 10240 | bytes 81920 | tf_op jit(solution)/shard_map/psum | solution.py:146
  92.5 0.7 select_bitcast_fusion
  (31 shorter events, 0.3 us)
Async XLA Ops:
  0.6 8.8 %copy-start = (bf16[1280,960]{0,1:T(8,128)(2,1)S(1)}, bf16[1280,960]{0,1:T(8,128)(2,1)}, u32[]{:S(2)}) copy-start(bf16[1280,960]{0,1:T(8,128)(2,1)} %param.17) | copy-start | bytes 7372804
  0.6 10.8 %copy-start.6 = (s32[1,11]{1,0:T(1,128)S(1)}, s32[1,11]{1,0:T(1,128)}, u32[]{:S(2)}) copy-start(s32[1,11]{1,0:T(1,128)} %param.27) | copy-start | bytes 136
  0.7 10.8 %copy-start.1 = (s32[32]{0:T(128)S(1)}, s32[32]{0:T(128)}, u32[]{:S(2)}) copy-start(s32[32]{0:T(128)} %param.25) | copy-start | bytes 388
  37.6 13.3 %copy-start.4 = (s32[32]{0:T(128)S(1)}, s32[32]{0:T(128)}, u32[]{:S(2)}) copy-start(s32[32]{0:T(128)} %param.24) | copy-start | bytes 388
  37.6 13.4 %copy-start.5 = (s32[32]{0:T(128)S(1)}, s32[32]{0:T(128)}, u32[]{:S(2)}) copy-start(s32[32]{0:T(128)} %param.23) | copy-start | bytes 388
  37.6 36.4 %copy-start.2 = (bf16[8,1280]{1,0:T(8,128)(2,1)S(1)}, bf16[8,1280]{1,0:T(8,128)(2,1)}, u32[]{:S(2)}) copy-start(bf16[8,1280]{1,0:T(8,128)(2,1)} %param.15) | copy-start | bytes 61444
  37.6 36.6 %copy-start.3 = (f32[1280]{0:T(1024)S(1)}, f32[1280]{0:T(1024)}, u32[]{:S(2)}) copy-start(f32[1280]{0:T(1024)} %param.19) | copy-start | bytes 15364
  49.3 3.6 %collective-permute-start = (bf16[8,320]{1,0:T(8,128)(2,1)S(1)}, bf16[8,320]{1,0:T(8,128)(2,1)S(1)}, u32[]{:S(2)}, u32[]{:S(2)}) collective-permute-start(bf16[8,320]{1,0:T(8,128)(2,1)S(1)} %reshape.204), channel_id=1, source_target_pairs={{0,16},{16,0},{1,17},{17,1},{2,18},{18,2},{3,19},{19,3},{4,20},{20... | collective-permute-start | bytes 15368 | tf_op jit(solution)/shard_map/ppermute | solution.py:28
where the time goes:
time: 93.8 us; the launch traced here: 93.2 us
  blocking collectives  58.8 us (63%)
  local copies, waits for them, and re-layouts  14 us (15%)
  matrix products  11.3 us (12%)
  other arithmetic  5.42 us (6%)
  starting transfers between devices  1.54 us (2%)
  waiting for transfers between devices  1.2 us (1%)
    psum x1, blocking collectives, body(): residual = token_state.astype(jnp.float32) + lax.psum(partial_out, 'tp')  19.7 us
    all_gather x3, blocking collectives, combined_all(): pieces = jax.tree.map(lambda part: lax.all_gather(part, axis), value)  16.6 us
    psum x1, blocking collectives, body(): lax.psum(jnp.dot(activated, down_weight, preferred_element_type=jnp.float...  16.1 us
    unnamed x17, local copies, waits for them, and re-layouts  10.4 us
    all_gather x1, blocking collectives, body(): lax.all_gather(token_state, 'kv', axis=0, tiled=True)  6.49 us
    dot_general x1, matrix products, body(): jnp.einsum('bth,bthd->bhd', weights.astype(jnp.bfloat16), blocks[:, :, :,...  3.09 us
    dot_general x1, matrix products, body(): jnp.einsum('bhd,bthd->bth', block_query, blocks[:, :, :, 0], preferred_el...  2.6 us
    dot_general x1, matrix products, body(): jnp.dot(activated, down_weight, preferred_element_type=jnp.float32)  2.14 us
  transfers between devices with their start and end apart: 1, of which 1 were waited for; matrix products, arithmetic and copies ran while one was open for 1% of the time, Pallas kernels for 0%

commit v1 on v0

v1 whole, which is shorter than its diff:
```python
import functools

import jax
import jax.numpy as jnp
from jax import lax
from jax.experimental import pallas as pl
from jax.experimental.pallas import tpu as pltpu
from jax.sharding import PartitionSpec as P

HD = 80
PAIR = 2 * HD

very_low = -1e30
norm_eps = 1e-06

MESH = pl.DeviceIdType.MESH
BF16 = jnp.bfloat16
F32 = jnp.float32


def root_norm(values_in, gain_vector):
    values_in = values_in.astype(F32)
    scaled = values_in * lax.rsqrt(
        jnp.mean(values_in * values_in, axis=-1, keepdims=True) + norm_eps
    )
    return scaled * gain_vector


def gelu_tanh(x):
    return 0.5 * x * (1.0 + jnp.tanh(0.7978845608028654 * (x + 0.044715 * (x * x * x))))


def dot_last(left, right):
    return lax.dot_general(left, right, (((1,), (1,)), ((), ())), preferred_element_type=F32)


def dot_plain(left, right):
    return lax.dot_general(left, right, (((1,), (0,)), ((), ())), preferred_element_type=F32)


def kernel(
    sizes,
    state_ref,
    attn_gain_ref,
    mlp_gain_ref,
    home_ref,
    moving_ref,
    length_ref,
    owner_ref,
    index_ref,
    qkv_hbm,
    out_hbm,
    up_hbm,
    down_hbm,
    cache_hbm,
    hidden_ref,
    entries_ref,
    w_query,
    w_pair,
    w_out,
    w_up,
    w_down,
    cache,
    q_all,
    q_rows,
    stat_send,
    sums_send,
    stat_recv,
    sums_recv,
    part_out,
    part_down,
    load_sem,
    cache_sem,
    q_send_sem,
    q_recv_sem,
    stat_send_sem,
    stat_recv_sem,
    sums_send_sem,
    sums_recv_sem,
    out_send_sem,
    out_recv_sem,
    down_send_sem,
    down_recv_sem,
):
    reps, kvs, tps, heads, blocks, tokens, rows, requests = sizes
    width = heads * PAIR
    sources = reps * kvs
    rep = lax.axis_index("rep")
    kv = lax.axis_index("kv")
    tp = lax.axis_index("tp")
    me = rep * kvs + kv

    def source_id(number):
        return {"rep": lax.div(number, kvs), "kv": lax.rem(number, kvs)}

    barrier = pltpu.get_barrier_semaphore()
    for step in range(1, sources):
        pl.semaphore_signal(
            barrier,
            inc=1,
            device_id=source_id(lax.rem(me + step, sources)),
            device_id_type=MESH,
        )
    for step in range(1, tps):
        pl.semaphore_signal(
            barrier, inc=1, device_id={"tp": lax.rem(tp + step, tps)}, device_id_type=MESH
        )

    query_loads, pair_loads, out_loads = [], [], []
    for h in range(heads):
        query_loads.append(
            pltpu.make_async_copy(
                qkv_hbm.at[pl.ds(h * 3 * HD, PAIR)],
                w_query.at[pl.ds(h * PAIR, PAIR)],
                load_sem.at[h],
            )
        )
        pair_loads.append(
            pltpu.make_async_copy(
                qkv_hbm.at[pl.ds(h * 3 * HD + HD, PAIR)],
                w_pair.at[pl.ds(h * PAIR, PAIR)],
                load_sem.at[heads + h],
            )
        )
        for half in range(2):
            out_loads.append(
                pltpu.make_async_copy(
                    out_hbm.at[pl.ds(h * HD, HD)],
                    w_out.at[pl.ds(h * PAIR + half * HD, HD)],
                    load_sem.at[2 * heads + 2 * h + half],
                )
            )
    up_load = pltpu.make_async_copy(up_hbm, w_up, load_sem.at[4 * heads])
    down_load = pltpu.make_async_copy(down_hbm, w_down, load_sem.at[4 * heads + 1])
    cache_loads = [
        pltpu.make_async_copy(cache_hbm.at[0, b], cache.at[b], cache_sem.at[b])
        for b in range(blocks)
    ]
    for copy in query_loads + cache_loads + pair_loads + out_loads + [up_load, down_load]:
        copy.start()

    state = state_ref[...].astype(F32)
    normed = root_norm(state, attn_gain_ref[...]).astype(BF16)
    for copy in query_loads:
        copy.wait()
    query = (dot_last(normed, w_query[...]) * HD ** (-0.5)).astype(BF16)
    q_all[kv] = query

    pl.semaphore_wait(barrier, sources - 1 + tps - 1)

    q_sends = []
    for step in range(1, kvs):
        copy = pltpu.make_async_remote_copy(
            src_ref=q_all.at[kv],
            dst_ref=q_all.at[kv],
            send_sem=q_send_sem.at[step],
            recv_sem=q_recv_sem.at[kv],
            device_id={"kv": lax.rem(kv + step, kvs)},
            device_id_type=MESH,
        )
        copy.start()
        q_sends.append(copy)

    for copy in pair_loads:
        copy.wait()
    pairs = dot_last(normed, w_pair[...])
    fresh = pairs.astype(BF16).astype(F32)
    lane = lax.broadcasted_iota(jnp.int32, (1, width), 1)
    lane_head = sum((lane >= h * PAIR).astype(jnp.int32) for h in range(1, heads))
    is_value = (lane - lane_head * PAIR) >= HD
    small_lane = lax.broadcasted_iota(jnp.int32, (1, 128), 1)
    self_products = jnp.where(is_value, 0.0, query.astype(F32) * fresh)
    self_score = jnp.full((rows, 128), very_low, F32)
    for h in range(heads):
        score = jnp.sum(jnp.where(lane_head == h, self_products, 0.0), axis=1, keepdims=True)
        self_score = jnp.where(small_lane == h, score, self_score)
    fresh_values = jnp.where(is_value, fresh, 0.0)

    row_number = lax.broadcasted_iota(jnp.int32, (rows, 1), 0)
    target = jnp.zeros((rows, 1), jnp.int32)
    for i in range(rows):
        slot = kv * rows + i
        aim = jnp.bitwise_xor(home_ref[slot], moving_ref[slot])
        target = jnp.where(row_number == i, aim, target)
    served_here = target == rep
    entries_ref[0] = jnp.where(served_here, pairs, 0.0)

    for step in range(1, kvs):
        other = lax.rem(kv + step, kvs)
        pltpu.make_async_remote_copy(
            src_ref=q_all.at[other],
            dst_ref=q_all.at[other],
            send_sem=q_send_sem.at[step],
            recv_sem=q_recv_sem.at[other],
            device_id={"kv": other},
            device_id_type=MESH,
        ).wait_recv()
    q_rows[...] = q_all[...].astype(F32).reshape(requests, width)

    head_row = lax.broadcasted_iota(jnp.int32, (8, 1), 0)
    key_mask = (lane_head == head_row) & ~is_value
    value_mask = (lane_head == head_row) & is_value
    token_lane = lax.broadcasted_iota(jnp.int32, (1, tokens), 1)

    owners, limits, scores, peaks = [], [], [], []
    for b in range(blocks):
        owner = owner_ref[0, b]
        clipped = jnp.minimum(owner, requests - 1)
        limit = jnp.where(
            owner < requests, length_ref[clipped] - index_ref[0, b] * tokens, 0
        )
        q_row = q_rows[pl.ds(clipped, 1), :]
        block_query = jnp.where(key_mask, q_row, 0.0).astype(BF16)
        cache_loads[b].wait()
        score = dot_last(block_query, cache[b])
        score = jnp.where(token_lane < limit, score, very_low)
        owners.append(owner)
        limits.append(limit)
        scores.append(score)
        peaks.append(jnp.max(score, axis=1, keepdims=True))

    slot_row = lax.broadcasted_iota(jnp.int32, (requests, 1), 0)
    sums = jnp.zeros((requests, width), F32)
    stats = jnp.where(small_lane < 8, very_low, 0.0) + jnp.zeros((requests, 128), F32)
    for b in range(blocks):
        shift = peaks[b]
        for other in range(blocks):
            if other != b:
                shift = jnp.where(
                    owners[other] == owners[b], jnp.maximum(shift, peaks[other]), shift
                )
        weight = jnp.where(token_lane < limits[b], jnp.exp(scores[b] - shift), 0.0)
        total = jnp.sum(weight, axis=1, keepdims=True)
        acc = dot_plain(weight.astype(BF16), cache[b])
        acc_row = jnp.sum(jnp.where(value_mask, acc, 0.0), axis=0, keepdims=True)
        stat_row = jnp.sum(
            jnp.where(
                small_lane == head_row, shift, jnp.where(small_lane == head_row + 8, total, 0.0)
            ),
            axis=0,
            keepdims=True,
        )
        mine = slot_row == owners[b]
        sums = sums + jnp.where(mine, acc_row, 0.0)
        stats = jnp.where(
            mine, jnp.where(small_lane < 8, stat_row, stats + stat_row), stats
        )
    stat_send[...] = stats.reshape(kvs, rows, 128)
    sums_send[...] = sums.reshape(kvs, rows, width).astype(BF16)

    partial_sends = []
    for step in range(1, sources):
        to = lax.rem(me + step, sources)
        to_kv = lax.rem(to, kvs)
        for src, dst, send_sem, recv_sem in (
            (stat_send, stat_recv, stat_send_sem, stat_recv_sem),
            (sums_send, sums_recv, sums_send_sem, sums_recv_sem),
        ):
            copy = pltpu.make_async_remote_copy(
                src_ref=src.at[to_kv],
                dst_ref=dst.at[me],
                send_sem=send_sem.at[step],
                recv_sem=recv_sem.at[me],
                device_id=source_id(to),
                device_id_type=MESH,
            )
            copy.start()
            partial_sends.append(copy)
    stat_recv[me] = stat_send[kv]
    sums_recv[me] = sums_send[kv]
    for step in range(1, sources):
        other = lax.rem(me + step, sources)
        for dst, send_sem, recv_sem in (
            (stat_recv, stat_send_sem, stat_recv_sem),
            (sums_recv, sums_send_sem, sums_recv_sem),
        ):
            pltpu.make_async_remote_copy(
                src_ref=dst.at[other],
                dst_ref=dst.at[other],
                send_sem=send_sem.at[step],
                recv_sem=recv_sem.at[other],
                device_id=source_id(other),
                device_id_type=MESH,
            ).wait_recv()

    def over_lanes(values):
        wide = jnp.broadcast_to(values[:, heads - 1 : heads], (rows, width))
        for h in reversed(range(heads - 1)):
            wide = jnp.where(lane < (h + 1) * PAIR, values[:, h : h + 1], wide)
        return wide

    top = self_score
    for s in range(sources):
        top = jnp.maximum(top, stat_recv[s])
    in_heads = small_lane < heads
    self_weight = jnp.exp(self_score - top)
    denominator = self_weight
    factors = []
    for s in range(sources):
        stat = stat_recv[s]
        factor = jnp.exp(stat - top)
        factors.append(factor)
        denominator = denominator + pltpu.roll(stat, 120, 1) * factor
    denominator = jnp.where(in_heads, denominator, 1.0)
    numerator = over_lanes(self_weight.astype(BF16).astype(F32)) * fresh_values
    for s in range(sources):
        numerator = numerator + over_lanes(factors[s]) * sums_recv[s].astype(F32)
    attended = (numerator / over_lanes(denominator)).astype(BF16)

    def summed_over_tp(part, buffer, send_sem, recv_sem):
        buffer[tp] = part.astype(BF16)
        sends = []
        for step in range(1, tps):
            copy = pltpu.make_async_remote_copy(
                src_ref=buffer.at[tp],
                dst_ref=buffer.at[tp],
                send_sem=send_sem.at[step],
                recv_sem=recv_sem.at[tp],
                device_id={"tp": lax.rem(tp + step, tps)},
                device_id_type=MESH,
            )
            copy.start()
            sends.append(copy)
        for step in range(1, tps):
            other = lax.rem(tp + step, tps)
            pltpu.make_async_remote_copy(
                src_ref=buffer.at[other],
                dst_ref=buffer.at[other],
                send_sem=send_sem.at[step],
                recv_sem=recv_sem.at[other],
                device_id={"tp": other},
                device_id_type=MESH,
            ).wait_recv()
        total = buffer[0].astype(F32)
        for t in range(1, tps):
            total = total + buffer[t].astype(F32)
        return total, sends

    for copy in out_loads:
        copy.wait()
    attn_out, out_sends = summed_over_tp(
        dot_plain(attended, w_out[...]), part_out, out_send_sem, out_recv_sem
    )
    residual = state + attn_out
    normed_mlp = root_norm(residual, mlp_gain_ref[...]).astype(BF16)
    up_load.wait()
    activated = gelu_tanh(dot_last(normed_mlp, w_up[...])).astype(BF16)
    down_load.wait()
    mlp_out, down_sends = summed_over_tp(
        dot_plain(activated, w_down[...]), part_down, down_send_sem, down_recv_sem
    )
    hidden_ref[0] = jnp.where(served_here, residual + mlp_out, 0.0)
    for copy in q_sends + partial_sends + out_sends + down_sends:
        copy.wait_send()


def body(
    reps,
    kvs,
    tps,
    token_state,
    attn_gain,
    qkv_weight,
    out_weight,
    mlp_gain,
    up_weight,
    down_weight,
    kv_cache,
    home_replica,
    moving,
    cache_length,
    block_owner,
    block_index,
):
    rows, model = token_state.shape
    requests = home_replica.shape[0]
    heads = out_weight.shape[0] // HD
    hidden_units = down_weight.shape[0]
    _, blocks, tokens, width = kv_cache.shape
    sources = reps * kvs
    sizes = (reps, kvs, tps, heads, blocks, tokens, rows, requests)
    vmem = pl.BlockSpec(memory_space=pltpu.VMEM)
    smem = pl.BlockSpec(memory_space=pltpu.SMEM)
    anywhere = pl.BlockSpec(memory_space=pl.ANY)
    dma = pltpu.SemaphoreType.DMA
    return pl.pallas_call(
        functools.partial(kernel, sizes),
        out_shape=(
            jax.ShapeDtypeStruct((1, rows, model), F32),
            jax.ShapeDtypeStruct((1, rows, width), F32),
        ),
        in_specs=[vmem] * 3 + [smem] * 5 + [anywhere] * 5,
        out_specs=(vmem, vmem),
        scratch_shapes=[
            pltpu.VMEM((width, model), BF16),
            pltpu.VMEM((width, model), BF16),
            pltpu.VMEM((width, model), BF16),
            pltpu.VMEM((hidden_units, model), BF16),
            pltpu.VMEM((hidden_units, model), BF16),
            pltpu.VMEM((blocks, tokens, width), BF16),
            pltpu.VMEM((kvs, rows, width), BF16),
            pltpu.VMEM((requests, width), F32),
            pltpu.VMEM((kvs, rows, 128), F32),
            pltpu.VMEM((kvs, rows, width), BF16),
            pltpu.VMEM((sources, rows, 128), F32),
            pltpu.VMEM((sources, rows, width), BF16),
            pltpu.VMEM((tps, rows, model), BF16),
            pltpu.VMEM((tps, rows, model), BF16),
            dma((4 * heads + 2,)),
            dma((blocks,)),
            dma((kvs,)),
            dma((kvs,)),
            dma((sources,)),
            dma((sources,)),
            dma((sources,)),
            dma((sources,)),
            dma((tps,)),
            dma((tps,)),
            dma((tps,)),
            dma((tps,)),
        ],
        compiler_params=pltpu.CompilerParams(
            collective_id=0, has_side_effects=True, vmem_limit_bytes=56 * 1024 * 1024
        ),
        name="decode_layer",
    )(
        token_state,
        attn_gain.reshape(1, model),
        mlp_gain.reshape(1, model),
        home_replica,
        moving,
        cache_length,
        block_owner,
        block_index,
        qkv_weight.T,
        out_weight,
        up_weight.T,
        down_weight,
        kv_cache,
    )


def solution(mesh):
    return jax.shard_map(
        functools.partial(body, mesh.shape["rep"], mesh.shape["kv"], mesh.shape["tp"]),
        mesh=mesh,
        in_specs=(
            P("kv", None),
            P(),
            P(None, "tp"),
            P("tp", None),
            P(),
            P(None, "tp"),
            P("tp", None),
            P("rep", "kv", None, "tp"),
            P(),
            P(),
            P(),
            P("rep", "kv"),
            P("rep", "kv"),
        ),
        out_specs=(P("rep", "kv", None), P("rep", "kv", "tp")),
        check_vma=False,
    )
```

time: 93.8 us -> 34.6 us (0.37)
  blocking collectives: 58.8 us -> 0 us
  Pallas kernels: 0 us -> 28.2 us
  matrix products: 11.3 us -> 0 us
  local copies, waits for them, and re-layouts: 14 us -> 5.32 us
  other arithmetic: 5.42 us -> 0 us
  starting transfers between devices: 1.54 us -> 0 us
  waiting for transfers between devices: 1.2 us -> 0 us
    psum x2 -> x0, blocking collectives: 35.8 us -> none  [the longest x1 19.7 us: body(): residual = token_state.astype(jnp.float32) + lax.psum(partial_out, 'tp')]
    pallas_call x0 -> x1, Pallas kernels: none -> 28.2 us  [body(): pl.pallas_call(functools.partial(kernel, sizes), out_shape=(jax.ShapeDtyp...]
    all_gather x4 -> x0, blocking collectives: 23 us -> none  [the longest x3 16.6 us: combined_all(): pieces = jax.tree.map(lambda part: lax.all_gather(part, axis), value)]
    dot_general x7 -> x0, matrix products: 11.3 us -> none  [the longest x1 3.09 us: body(): jnp.einsum('bth,bthd->bhd', weights.astype(jnp.bfloat16), blocks[:, :, :,...]
    unnamed x17 -> x2, local copies, waits for them, and re-layouts: 10.4 us -> 2.73 us
    reshape x3 -> x2, local copies, waits for them, and re-layouts: 0.48 us -> 2.59 us  [the longest x1 1.29 us: body(): attn_gain.reshape(1, model)]
    gather x3 -> x0, local copies, waits for them, and re-layouts: 1.8 us -> none  [the longest x1 0.66 us: body(): usable = is_owned[:, None] & (positions < cache_length[clipped][:, None])]
    ppermute x1 -> x0, starting transfers between devices: 1.54 us -> none  [from_partner(): return lax.ppermute(block, axis, route)]
  transfers between devices with their start and end apart: 1 -> 0, of which waited for: 1 -> 0; matrix products, arithmetic and copies ran while one was open for 1% -> 0% of each run, Pallas kernels for 0% -> 0%
where the time goes in v1:
time: 34.6 us; the launch traced here: 34.2 us
  Pallas kernels  28.2 us (82%)
  local copies, waits for them, and re-layouts  5.32 us (15%)
  between operations  0.64 us (2%)
    pallas_call x1, Pallas kernels, body(): pl.pallas_call(functools.partial(kernel, sizes), out_shape=(jax.ShapeDtyp...  28.2 us
    unnamed x2, local copies, waits for them, and re-layouts  2.73 us
    reshape x1, local copies, waits for them, and re-layouts, body(): attn_gain.reshape(1, model)  1.29 us
    reshape x1, local copies, waits for them, and re-layouts, body(): mlp_gain.reshape(1, model)  1.29 us

profile of v1, /device:TPU:0, one launch (start us, length us, event | category | flops | bytes accessed | tf_op | source)
XLA Modules:
  0.0 34.2 jit_solution(3612972383748123192)
XLA Ops:
  0.6 1.3 %reshape.10.attn_gain_ref = f32[1,1280]{1,0:T(1,128)} reshape(f32[1280]{0:T(1024)} %param.14) | data formatting | bytes 10240 | tf_op jit(solution)/shard_map/reshape | solution.py:428
  1.9 1.3 %reshape.11.mlp_gain_ref = f32[1,1280]{1,0:T(1,128)} reshape(f32[1280]{0:T(1024)} %param.17) | data formatting | bytes 10240 | tf_op jit(solution)/shard_map/reshape | solution.py:429
  3.2 28.2 %decode_layer.1 = (f32[1,8,1280]{2,1,0:T(8,128)}, f32[1,8,640]{2,1,0:T(8,128)}) custom-call(bf16[8,1280]{1,0:T(8,128)(2,1)} %state_ref.1, f32[1,1280]{1,0:T(1,128)} %reshape.10.attn_gain_ref, f32[1,1280]{1,0:T(1,128)} %reshape.11.mlp_gain_ref, s32[32]{0:T(128)} %home_ref.1, s32[32]{0:T(128)} %moving_ref.1, s32[32]{0:T(128)} %length_ref.1, ...), custom_call_target="tpu_custom_call" | custom-call | tf_op jit(solution)/shard_map/decode_layer/pallas_call | solution.py:386
  31.5 1.4 %copy.17 = f32[1,8,1280]{2,1,0:T(8,128)} copy(f32[1,8,1280]{2,1,0:T(8,128)} %get-tuple-element.4) | data formatting | bytes 81920
  32.9 1.3 %copy.18 = f32[1,8,640]{2,1,0:T(8,128)} copy(f32[1,8,640]{2,1,0:T(8,128)} %get-tuple-element.5) | data formatting | bytes 40960

commit v2 on v1

--- a/solution.py
+++ b/solution.py
@@ -106,12 +106,12 @@
             barrier, inc=1, device_id={"tp": lax.rem(tp + step, tps)}, device_id_type=MESH
         )
 
-    query_loads, pair_loads, out_loads = [], [], []
+    query_loads, pair_loads = [], []
     for h in range(heads):
         query_loads.append(
             pltpu.make_async_copy(
-                qkv_hbm.at[pl.ds(h * 3 * HD, PAIR)],
-                w_query.at[pl.ds(h * PAIR, PAIR)],
+                qkv_hbm.at[pl.ds(h * 3 * HD, HD)],
+                w_query.at[pl.ds(h * HD, HD)],
                 load_sem.at[h],
             )
         )
@@ -122,28 +122,26 @@
                 load_sem.at[heads + h],
             )
         )
-        for half in range(2):
-            out_loads.append(
-                pltpu.make_async_copy(
-                    out_hbm.at[pl.ds(h * HD, HD)],
-                    w_out.at[pl.ds(h * PAIR + half * HD, HD)],
-                    load_sem.at[2 * heads + 2 * h + half],
-                )
-            )
-    up_load = pltpu.make_async_copy(up_hbm, w_up, load_sem.at[4 * heads])
-    down_load = pltpu.make_async_copy(down_hbm, w_down, load_sem.at[4 * heads + 1])
+    out_load = pltpu.make_async_copy(out_hbm, w_out, load_sem.at[2 * heads])
+    up_load = pltpu.make_async_copy(up_hbm, w_up, load_sem.at[2 * heads + 1])
+    down_load = pltpu.make_async_copy(down_hbm, w_down, load_sem.at[2 * heads + 2])
     cache_loads = [
         pltpu.make_async_copy(cache_hbm.at[0, b], cache.at[b], cache_sem.at[b])
         for b in range(blocks)
     ]
-    for copy in query_loads + cache_loads + pair_loads + out_loads + [up_load, down_load]:
+    for copy in query_loads + cache_loads + pair_loads + [out_load, up_load, down_load]:
         copy.start()
 
     state = state_ref[...].astype(F32)
-    normed = root_norm(state, attn_gain_ref[...]).astype(BF16)
+    normed = root_norm(state, attn_gain_ref[...].reshape(1, -1)).astype(BF16)
     for copy in query_loads:
         copy.wait()
-    query = (dot_last(normed, w_query[...]) * HD ** (-0.5)).astype(BF16)
+    compact = dot_last(normed, w_query[...]) * HD ** (-0.5)
+    gap = jnp.zeros((rows, HD), F32)
+    spread = []
+    for h in range(heads):
+        spread += [compact[:, h * HD : (h + 1) * HD], gap]
+    query = jnp.concatenate(spread, axis=1).astype(BF16)
     q_all[kv] = query
 
     pl.semaphore_wait(barrier, sources - 1 + tps - 1)
@@ -202,6 +200,8 @@
     value_mask = (lane_head == head_row) & is_value
     token_lane = lax.broadcasted_iota(jnp.int32, (1, tokens), 1)
 
+    for copy in cache_loads:
+        copy.wait()
     owners, limits, scores, peaks = [], [], [], []
     for b in range(blocks):
         owner = owner_ref[0, b]
@@ -211,7 +211,6 @@
         )
         q_row = q_rows[pl.ds(clipped, 1), :]
         block_query = jnp.where(key_mask, q_row, 0.0).astype(BF16)
-        cache_loads[b].wait()
         score = dot_last(block_query, cache[b])
         score = jnp.where(token_lane < limit, score, very_low)
         owners.append(owner)
@@ -305,7 +304,10 @@
     numerator = over_lanes(self_weight.astype(BF16).astype(F32)) * fresh_values
     for s in range(sources):
         numerator = numerator + over_lanes(factors[s]) * sums_recv[s].astype(F32)
-    attended = (numerator / over_lanes(denominator)).astype(BF16)
+    attended = numerator / over_lanes(denominator)
+    attended = jnp.concatenate(
+        [attended[:, h * PAIR + HD : (h + 1) * PAIR] for h in range(heads)], axis=1
+    ).astype(BF16)
 
     def summed_over_tp(part, buffer, send_sem, recv_sem):
         buffer[tp] = part.astype(BF16)
@@ -336,13 +338,12 @@
             total = total + buffer[t].astype(F32)
         return total, sends
 
-    for copy in out_loads:
-        copy.wait()
+    out_load.wait()
     attn_out, out_sends = summed_over_tp(
         dot_plain(attended, w_out[...]), part_out, out_send_sem, out_recv_sem
     )
     residual = state + attn_out
-    normed_mlp = root_norm(residual, mlp_gain_ref[...]).astype(BF16)
+    normed_mlp = root_norm(residual, mlp_gain_ref[...].reshape(1, -1)).astype(BF16)
     up_load.wait()
     activated = gelu_tanh(dot_last(normed_mlp, w_up[...])).astype(BF16)
     down_load.wait()
@@ -386,15 +387,15 @@
     return pl.pallas_call(
         functools.partial(kernel, sizes),
         out_shape=(
-            jax.ShapeDtypeStruct((1, rows, model), F32),
-            jax.ShapeDtypeStruct((1, rows, width), F32),
+            pltpu.VMEM((1, rows, model), F32),
+            pltpu.VMEM((1, rows, width), F32),
         ),
         in_specs=[vmem] * 3 + [smem] * 5 + [anywhere] * 5,
         out_specs=(vmem, vmem),
         scratch_shapes=[
+            pltpu.VMEM((heads * HD, model), BF16),
             pltpu.VMEM((width, model), BF16),
-            pltpu.VMEM((width, model), BF16),
-            pltpu.VMEM((width, model), BF16),
+            pltpu.VMEM((heads * HD, model), BF16),
             pltpu.VMEM((hidden_units, model), BF16),
             pltpu.VMEM((hidden_units, model), BF16),
             pltpu.VMEM((blocks, tokens, width), BF16),
@@ -406,7 +407,7 @@
             pltpu.VMEM((sources, rows, width), BF16),
             pltpu.VMEM((tps, rows, model), BF16),
             pltpu.VMEM((tps, rows, model), BF16),
-            dma((4 * heads + 2,)),
+            dma((2 * heads + 3,)),
             dma((blocks,)),
             dma((kvs,)),
             dma((kvs,)),
@@ -425,8 +426,8 @@
         name="decode_layer",
     )(
         token_state,
-        attn_gain.reshape(1, model),
-        mlp_gain.reshape(1, model),
+        attn_gain,
+        mlp_gain,
         home_replica,
         moving,
         cache_length,

time: 34.6 us -> 27.7 us (0.80)
  local copies, waits for them, and re-layouts: 5.32 us -> 1.23 us
  Pallas kernels: 28.2 us -> 25.6 us
    pallas_call x1, Pallas kernels: 28.2 us -> 25.6 us  [body(): pl.pallas_call(functools.partial(kernel, sizes), out_shape=(pltpu.VMEM((1...]
    reshape x2 -> x0, local copies, waits for them, and re-layouts: 2.59 us -> none  [the longest x1 1.29 us: body(): attn_gain.reshape(1, model)]
    unnamed x2, local copies, waits for them, and re-layouts: 2.73 us -> 1.23 us
where the time goes in v2:
time: 27.7 us; the launch traced here: 27.5 us
  Pallas kernels  25.6 us (92%)
  local copies, waits for them, and re-layouts  1.23 us (4%)
  between operations  0.64 us (2%)
    pallas_call x1, Pallas kernels, body(): pl.pallas_call(functools.partial(kernel, sizes), out_shape=(pltpu.VMEM((1...  25.6 us
    unnamed x2, local copies, waits for them, and re-layouts  1.23 us

profile of v2, /device:TPU:0, one launch (start us, length us, event | category | flops | bytes accessed | tf_op | source)
XLA Modules:
  0.0 27.5 jit_solution(11302995436470362951)
XLA Ops:
  0.6 25.6 %decode_layer.1 = (f32[1,8,1280]{2,1,0:T(8,128)S(1)}, f32[1,8,640]{2,1,0:T(8,128)S(1)}) custom-call(bf16[8,1280]{1,0:T(8,128)(2,1)} %state_ref.1, f32[1280]{0:T(1024)} %attn_gain_ref.1, f32[1280]{0:T(1024)} %mlp_gain_ref.1, s32[32]{0:T(128)} %home_ref.1, s32[32]{0:T(128)} %moving_ref.1, s32[32]{0:T(128)} %length_ref.1, s32[1,11]{1,0:T(1,128)} %owner_ref.1, ...), custom_call_target="tpu_custom_call" | custom-call | tf_op jit(solution)/shard_map/decode_layer/pallas_call | solution.py:387
  26.3 0.6 %copy.17 = f32[1,8,1280]{2,1,0:T(8,128)} copy(f32[1,8,1280]{2,1,0:T(8,128)S(1)} %get-tuple-element.2) | data formatting | bytes 81920
  26.9 0.6 %copy.18 = f32[1,8,640]{2,1,0:T(8,128)} copy(f32[1,8,640]{2,1,0:T(8,128)S(1)} %get-tuple-element.3) | data formatting | bytes 40960

commit v3 on v2

--- a/solution.py
+++ b/solution.py
@@ -40,6 +40,21 @@
 
 def kernel(
     sizes,
+    state_hbm,
+    attn_gain_hbm,
+    mlp_gain_hbm,
+    home_hbm,
+    moving_hbm,
+    length_hbm,
+    owner_hbm,
+    index_hbm,
+    qkv_hbm,
+    out_hbm,
+    up_hbm,
+    down_hbm,
+    cache_hbm,
+    hidden_ref,
+    entries_ref,
     state_ref,
     attn_gain_ref,
     mlp_gain_ref,
@@ -48,13 +63,6 @@
     length_ref,
     owner_ref,
     index_ref,
-    qkv_hbm,
-    out_hbm,
-    up_hbm,
-    down_hbm,
-    cache_hbm,
-    hidden_ref,
-    entries_ref,
     w_query,
     w_pair,
     w_out,
@@ -69,6 +77,7 @@
     sums_recv,
     part_out,
     part_down,
+    small_sem,
     load_sem,
     cache_sem,
     q_send_sem,
@@ -106,6 +115,21 @@
             barrier, inc=1, device_id={"tp": lax.rem(tp + step, tps)}, device_id_type=MESH
         )
 
+    small_loads = [
+        pltpu.make_async_copy(source, held, small_sem.at[i])
+        for i, (source, held) in enumerate(
+            (
+                (state_hbm, state_ref),
+                (attn_gain_hbm, attn_gain_ref),
+                (mlp_gain_hbm, mlp_gain_ref),
+                (home_hbm, home_ref),
+                (moving_hbm, moving_ref),
+                (length_hbm, length_ref),
+                (owner_hbm, owner_ref),
+                (index_hbm, index_ref),
+            )
+        )
+    ]
     query_loads, pair_loads = [], []
     for h in range(heads):
         query_loads.append(
@@ -129,8 +153,12 @@
         pltpu.make_async_copy(cache_hbm.at[0, b], cache.at[b], cache_sem.at[b])
         for b in range(blocks)
     ]
-    for copy in query_loads + cache_loads + pair_loads + [out_load, up_load, down_load]:
+    for copy in small_loads[:2] + query_loads + small_loads[2:] + cache_loads:
         copy.start()
+    for copy in pair_loads + [out_load, up_load, down_load]:
+        copy.start()
+    for copy in small_loads[:2]:
+        copy.wait()
 
     state = state_ref[...].astype(F32)
     normed = root_norm(state, attn_gain_ref[...].reshape(1, -1)).astype(BF16)
@@ -159,30 +187,12 @@
         copy.start()
         q_sends.append(copy)
 
-    for copy in pair_loads:
-        copy.wait()
-    pairs = dot_last(normed, w_pair[...])
-    fresh = pairs.astype(BF16).astype(F32)
     lane = lax.broadcasted_iota(jnp.int32, (1, width), 1)
     lane_head = sum((lane >= h * PAIR).astype(jnp.int32) for h in range(1, heads))
     is_value = (lane - lane_head * PAIR) >= HD
     small_lane = lax.broadcasted_iota(jnp.int32, (1, 128), 1)
-    self_products = jnp.where(is_value, 0.0, query.astype(F32) * fresh)
-    self_score = jnp.full((rows, 128), very_low, F32)
-    for h in range(heads):
-        score = jnp.sum(jnp.where(lane_head == h, self_products, 0.0), axis=1, keepdims=True)
-        self_score = jnp.where(small_lane == h, score, self_score)
-    fresh_values = jnp.where(is_value, fresh, 0.0)
-
-    row_number = lax.broadcasted_iota(jnp.int32, (rows, 1), 0)
-    target = jnp.zeros((rows, 1), jnp.int32)
-    for i in range(rows):
-        slot = kv * rows + i
-        aim = jnp.bitwise_xor(home_ref[slot], moving_ref[slot])
-        target = jnp.where(row_number == i, aim, target)
-    served_here = target == rep
-    entries_ref[0] = jnp.where(served_here, pairs, 0.0)
-
+    for copy in small_loads[2:]:
+        copy.wait()
     for step in range(1, kvs):
         other = lax.rem(kv + step, kvs)
         pltpu.make_async_remote_copy(
@@ -267,6 +277,27 @@
             partial_sends.append(copy)
     stat_recv[me] = stat_send[kv]
     sums_recv[me] = sums_send[kv]
+
+    for copy in pair_loads:
+        copy.wait()
+    pairs = dot_last(normed, w_pair[...])
+    fresh = pairs.astype(BF16).astype(F32)
+    self_products = jnp.where(is_value, 0.0, query.astype(F32) * fresh)
+    self_score = jnp.full((rows, 128), very_low, F32)
+    for h in range(heads):
+        score = jnp.sum(jnp.where(lane_head == h, self_products, 0.0), axis=1, keepdims=True)
+        self_score = jnp.where(small_lane == h, score, self_score)
+    fresh_values = jnp.where(is_value, fresh, 0.0)
+
+    row_number = lax.broadcasted_iota(jnp.int32, (rows, 1), 0)
+    target = jnp.zeros((rows, 1), jnp.int32)
+    for i in range(rows):
+        slot = kv * rows + i
+        aim = jnp.bitwise_xor(home_ref[slot], moving_ref[slot])
+        target = jnp.where(row_number == i, aim, target)
+    served_here = target == rep
+    entries_ref[0] = jnp.where(served_here, pairs, 0.0)
+
     for step in range(1, sources):
         other = lax.rem(me + step, sources)
         for dst, send_sem, recv_sem in (
@@ -355,6 +386,17 @@
         copy.wait_send()
 
 
+def write_results(hidden_in, entries_in, hidden_out, entries_out, sem):
+    copies = [
+        pltpu.make_async_copy(hidden_in, hidden_out, sem.at[0]),
+        pltpu.make_async_copy(entries_in, entries_out, sem.at[1]),
+    ]
+    for copy in copies:
+        copy.start()
+    for copy in copies:
+        copy.wait()
+
+
 def body(
     reps,
     kvs,
@@ -381,18 +423,25 @@
     sources = reps * kvs
     sizes = (reps, kvs, tps, heads, blocks, tokens, rows, requests)
     vmem = pl.BlockSpec(memory_space=pltpu.VMEM)
-    smem = pl.BlockSpec(memory_space=pltpu.SMEM)
     anywhere = pl.BlockSpec(memory_space=pl.ANY)
     dma = pltpu.SemaphoreType.DMA
-    return pl.pallas_call(
+    results = pl.pallas_call(
         functools.partial(kernel, sizes),
         out_shape=(
             pltpu.VMEM((1, rows, model), F32),
             pltpu.VMEM((1, rows, width), F32),
         ),
-        in_specs=[vmem] * 3 + [smem] * 5 + [anywhere] * 5,
+        in_specs=[anywhere] * 13,
         out_specs=(vmem, vmem),
         scratch_shapes=[
+            pltpu.VMEM((rows, model), BF16),
+            pltpu.VMEM((model,), F32),
+            pltpu.VMEM((model,), F32),
+            pltpu.SMEM((requests,), jnp.int32),
+            pltpu.SMEM((requests,), jnp.int32),
+            pltpu.SMEM((requests,), jnp.int32),
+            pltpu.SMEM((1, blocks), jnp.int32),
+            pltpu.SMEM((1, blocks), jnp.int32),
             pltpu.VMEM((heads * HD, model), BF16),
             pltpu.VMEM((width, model), BF16),
             pltpu.VMEM((heads * HD, model), BF16),
@@ -407,6 +456,7 @@
             pltpu.VMEM((sources, rows, width), BF16),
             pltpu.VMEM((tps, rows, model), BF16),
             pltpu.VMEM((tps, rows, model), BF16),
+            dma((8,)),
             dma((2 * heads + 3,)),
             dma((blocks,)),
             dma((kvs,)),
@@ -439,6 +489,17 @@
         down_weight,
         kv_cache,
     )
+    return pl.pallas_call(
+        write_results,
+        out_shape=(
+            jax.ShapeDtypeStruct((1, rows, model), F32),
+            jax.ShapeDtypeStruct((1, rows, width), F32),
+        ),
+        in_specs=[vmem] * 2,
+        out_specs=(anywhere, anywhere),
+        scratch_shapes=[dma((2,))],
+        name="write_results",
+    )(*results)
 
 
 def solution(mesh):

time: 27.7 us -> 28.6 us (1.032)
  Pallas kernels: 25.6 us -> 26.5 us
    pallas_call x0 -> x1, Pallas kernels: none -> 1.42 us  [body(): pl.pallas_call(write_results, out_shape=(jax.ShapeDtypeStruct((1, rows, m...]
    pallas_call x1, Pallas kernels: 25.6 us -> 25.1 us  [body(): pl.pallas_call(functools.partial(kernel, sizes), out_shape=(pltpu.VMEM((1...]
    unnamed x2 -> x4, local copies, waits for them, and re-layouts: 1.23 us -> 1.2 us
where the time goes in v3:
time: 28.6 us; the launch traced here: 28.4 us
  Pallas kernels  26.5 us (93%)
  local copies, waits for them, and re-layouts  1.2 us (4%)
  between operations  0.65 us (2%)
    pallas_call x1, Pallas kernels, body(): pl.pallas_call(functools.partial(kernel, sizes), out_shape=(pltpu.VMEM((1...  25.1 us
    pallas_call x1, Pallas kernels, body(): pl.pallas_call(write_results, out_shape=(jax.ShapeDtypeStruct((1, rows, m...  1.42 us
    unnamed x4, local copies, waits for them, and re-layouts  1.2 us

profile of v3, /device:TPU:0, one launch (start us, length us, event | category | flops | bytes accessed | tf_op | source)
XLA Modules:
  0.0 28.4 jit_solution(9360842156116872455)
XLA Ops:
  0.6 25.1 %decode_layer.1 = (f32[1,8,1280]{2,1,0:T(8,128)S(1)}, f32[1,8,640]{2,1,0:T(8,128)S(1)}) custom-call(bf16[8,1280]{1,0:T(8,128)(2,1)} %state_hbm.1, f32[1280]{0:T(1024)} %attn_gain_hbm.1, f32[1280]{0:T(1024)} %mlp_gain_hbm.1, s32[32]{0:T(128)} %home_hbm.1, s32[32]{0:T(128)} %moving_hbm.1, s32[32]{0:T(128)} %length_hbm.1, s32[1,11]{1,0:T(1,128)} %owner_hbm.1, ...), custom_call_target="tpu_custom_call" | custom-call | tf_op jit(solution)/shard_map/decode_layer/pallas_call | solution.py:428
  25.7 0.0 copy-start
  25.8 0.6 %copy-done = f32[1,8,1280]{2,1,0:T(8,128)} copy-done((f32[1,8,1280]{2,1,0:T(8,128)}, f32[1,8,1280]{2,1,0:T(8,128)S(1)}, u32[]{:S(2)}) %copy-start) | copy-done | bytes 40984
  26.4 0.0 copy-start.1
  26.4 0.6 %copy-done.1 = f32[1,8,640]{2,1,0:T(8,128)} copy-done((f32[1,8,640]{2,1,0:T(8,128)}, f32[1,8,640]{2,1,0:T(8,128)S(1)}, u32[]{:S(2)}) %copy-start.1) | copy-done | bytes 20504
  27.0 1.4 %write_results.1 = (f32[1,8,1280]{2,1,0:T(8,128)}, f32[1,8,640]{2,1,0:T(8,128)}) custom-call(f32[1,8,1280]{2,1,0:T(8,128)} %copy-done, f32[1,8,640]{2,1,0:T(8,128)} %copy-done.1), custom_call_target="tpu_custom_call" | custom-call | tf_op jit(solution)/shard_map/write_results/pallas_call | solution.py:492
Async XLA Ops:
  25.7 0.6 %copy-start = (f32[1,8,1280]{2,1,0:T(8,128)}, f32[1,8,1280]{2,1,0:T(8,128)S(1)}, u32[]{:S(2)}) copy-start(f32[1,8,1280]{2,1,0:T(8,128)S(1)} %get-tuple-element.4.hidden_in) | copy-start | bytes 122884
  26.4 0.6 %copy-start.1 = (f32[1,8,640]{2,1,0:T(8,128)}, f32[1,8,640]{2,1,0:T(8,128)S(1)}, u32[]{:S(2)}) copy-start(f32[1,8,640]{2,1,0:T(8,128)S(1)} %get-tuple-element.5.entries_in) | copy-start | bytes 61444

commit v4 on v3

--- a/solution.py
+++ b/solution.py
@@ -149,13 +149,14 @@
     out_load = pltpu.make_async_copy(out_hbm, w_out, load_sem.at[2 * heads])
     up_load = pltpu.make_async_copy(up_hbm, w_up, load_sem.at[2 * heads + 1])
     down_load = pltpu.make_async_copy(down_hbm, w_down, load_sem.at[2 * heads + 2])
+    middle = (blocks + 1) // 2
     cache_loads = [
-        pltpu.make_async_copy(cache_hbm.at[0, b], cache.at[b], cache_sem.at[b])
-        for b in range(blocks)
+        pltpu.make_async_copy(
+            cache_hbm.at[0, pl.ds(first, count)], cache.at[pl.ds(first, count)], cache_sem.at[i]
+        )
+        for i, (first, count) in enumerate(((0, middle), (middle, blocks - middle)))
     ]
-    for copy in small_loads[:2] + query_loads + small_loads[2:] + cache_loads:
-        copy.start()
-    for copy in pair_loads + [out_load, up_load, down_load]:
+    for copy in small_loads[:2] + query_loads + cache_loads:
         copy.start()
     for copy in small_loads[:2]:
         copy.wait()
@@ -186,6 +187,8 @@
         )
         copy.start()
         q_sends.append(copy)
+    for copy in small_loads[2:] + pair_loads + [out_load, up_load, down_load]:
+        copy.start()
 
     lane = lax.broadcasted_iota(jnp.int32, (1, width), 1)
     lane_head = sum((lane >= h * PAIR).astype(jnp.int32) for h in range(1, heads))
@@ -210,8 +213,6 @@
     value_mask = (lane_head == head_row) & is_value
     token_lane = lax.broadcasted_iota(jnp.int32, (1, tokens), 1)
 
-    for copy in cache_loads:
-        copy.wait()
     owners, limits, scores, peaks = [], [], [], []
     for b in range(blocks):
         owner = owner_ref[0, b]
@@ -219,6 +220,8 @@
         limit = jnp.where(
             owner < requests, length_ref[clipped] - index_ref[0, b] * tokens, 0
         )
+        if b in (0, middle):
+            cache_loads[b // middle].wait()
         q_row = q_rows[pl.ds(clipped, 1), :]
         block_query = jnp.where(key_mask, q_row, 0.0).astype(BF16)
         score = dot_last(block_query, cache[b])
@@ -331,11 +334,10 @@
         factor = jnp.exp(stat - top)
         factors.append(factor)
         denominator = denominator + pltpu.roll(stat, 120, 1) * factor
-    denominator = jnp.where(in_heads, denominator, 1.0)
-    numerator = over_lanes(self_weight.astype(BF16).astype(F32)) * fresh_values
+    share = 1.0 / jnp.where(in_heads, denominator, 1.0)
+    attended = over_lanes(self_weight.astype(BF16).astype(F32) * share) * fresh_values
     for s in range(sources):
-        numerator = numerator + over_lanes(factors[s]) * sums_recv[s].astype(F32)
-    attended = numerator / over_lanes(denominator)
+        attended = attended + over_lanes(factors[s] * share) * sums_recv[s].astype(F32)
     attended = jnp.concatenate(
         [attended[:, h * PAIR + HD : (h + 1) * PAIR] for h in range(heads)], axis=1
     ).astype(BF16)
@@ -386,17 +388,6 @@
         copy.wait_send()
 
 
-def write_results(hidden_in, entries_in, hidden_out, entries_out, sem):
-    copies = [
-        pltpu.make_async_copy(hidden_in, hidden_out, sem.at[0]),
-        pltpu.make_async_copy(entries_in, entries_out, sem.at[1]),
-    ]
-    for copy in copies:
-        copy.start()
-    for copy in copies:
-        copy.wait()
-
-
 def body(
     reps,
     kvs,
@@ -423,15 +414,15 @@
     sources = reps * kvs
     sizes = (reps, kvs, tps, heads, blocks, tokens, rows, requests)
     vmem = pl.BlockSpec(memory_space=pltpu.VMEM)
-    anywhere = pl.BlockSpec(memory_space=pl.ANY)
+    in_hbm = pl.BlockSpec(memory_space=pltpu.HBM)
     dma = pltpu.SemaphoreType.DMA
-    results = pl.pallas_call(
+    return pl.pallas_call(
         functools.partial(kernel, sizes),
         out_shape=(
             pltpu.VMEM((1, rows, model), F32),
             pltpu.VMEM((1, rows, width), F32),
         ),
-        in_specs=[anywhere] * 13,
+        in_specs=[in_hbm] * 13,
         out_specs=(vmem, vmem),
         scratch_shapes=[
             pltpu.VMEM((rows, model), BF16),
@@ -458,7 +449,7 @@
             pltpu.VMEM((tps, rows, model), BF16),
             dma((8,)),
             dma((2 * heads + 3,)),
-            dma((blocks,)),
+            dma((2,)),
             dma((kvs,)),
             dma((kvs,)),
             dma((sources,)),
@@ -489,17 +480,6 @@
         down_weight,
         kv_cache,
     )
-    return pl.pallas_call(
-        write_results,
-        out_shape=(
-            jax.ShapeDtypeStruct((1, rows, model), F32),
-            jax.ShapeDtypeStruct((1, rows, width), F32),
-        ),
-        in_specs=[vmem] * 2,
-        out_specs=(anywhere, anywhere),
-        scratch_shapes=[dma((2,))],
-        name="write_results",
-    )(*results)
 
 
 def solution(mesh):

time: 28.6 us -> 27.4 us (0.958)
  Pallas kernels: 26.5 us -> 25.4 us
    pallas_call x1 -> x0, Pallas kernels: 1.42 us -> none  [body(): pl.pallas_call(write_results, out_shape=(jax.ShapeDtypeStruct((1, rows, m...]
    pallas_call x1, Pallas kernels: 25.1 us -> 25.4 us  [body(): pl.pallas_call(functools.partial(kernel, sizes), out_shape=(pltpu.VMEM((1...]
    unnamed x4 -> x2, local copies, waits for them, and re-layouts: 1.2 us -> 1.23 us
where the time goes in v4:
time: 27.4 us; the launch traced here: 27.3 us
  Pallas kernels  25.4 us (93%)
  local copies, waits for them, and re-layouts  1.23 us (4%)
  between operations  0.64 us (2%)
    pallas_call x1, Pallas kernels, body(): pl.pallas_call(functools.partial(kernel, sizes), out_shape=(pltpu.VMEM((1...  25.4 us
    unnamed x2, local copies, waits for them, and re-layouts  1.23 us

profile of v4, /device:TPU:0, one launch (start us, length us, event | category | flops | bytes accessed | tf_op | source)
XLA Modules:
  0.0 27.3 jit_solution(1015141407048728307)
XLA Ops:
  0.6 25.4 %decode_layer.1 = (f32[1,8,1280]{2,1,0:T(8,128)S(1)}, f32[1,8,640]{2,1,0:T(8,128)S(1)}) custom-call(bf16[8,1280]{1,0:T(8,128)(2,1)} %state_hbm.1, f32[1280]{0:T(1024)} %attn_gain_hbm.1, f32[1280]{0:T(1024)} %mlp_gain_hbm.1, s32[32]{0:T(128)} %home_hbm.1, s32[32]{0:T(128)} %moving_hbm.1, s32[32]{0:T(128)} %length_hbm.1, s32[1,11]{1,0:T(1,128)} %owner_hbm.1, ...), custom_call_target="tpu_custom_call" | custom-call | tf_op jit(solution)/shard_map/decode_layer/pallas_call | solution.py:419
  26.1 0.6 %copy.17 = f32[1,8,1280]{2,1,0:T(8,128)} copy(f32[1,8,1280]{2,1,0:T(8,128)S(1)} %get-tuple-element.2) | data formatting | bytes 81920
  26.7 0.6 %copy.18 = f32[1,8,640]{2,1,0:T(8,128)} copy(f32[1,8,640]{2,1,0:T(8,128)S(1)} %get-tuple-element.3) | data formatting | bytes 40960

commit v5 on v4

--- a/solution.py
+++ b/solution.py
@@ -149,14 +149,13 @@
     out_load = pltpu.make_async_copy(out_hbm, w_out, load_sem.at[2 * heads])
     up_load = pltpu.make_async_copy(up_hbm, w_up, load_sem.at[2 * heads + 1])
     down_load = pltpu.make_async_copy(down_hbm, w_down, load_sem.at[2 * heads + 2])
-    middle = (blocks + 1) // 2
     cache_loads = [
-        pltpu.make_async_copy(
-            cache_hbm.at[0, pl.ds(first, count)], cache.at[pl.ds(first, count)], cache_sem.at[i]
-        )
-        for i, (first, count) in enumerate(((0, middle), (middle, blocks - middle)))
+        pltpu.make_async_copy(cache_hbm.at[0, b], cache.at[b], cache_sem.at[b])
+        for b in range(blocks)
     ]
-    for copy in small_loads[:2] + query_loads + cache_loads:
+    for copy in small_loads[:2] + query_loads + small_loads[2:] + cache_loads:
+        copy.start()
+    for copy in pair_loads + [out_load, up_load, down_load]:
         copy.start()
     for copy in small_loads[:2]:
         copy.wait()
@@ -187,8 +186,6 @@
         )
         copy.start()
         q_sends.append(copy)
-    for copy in small_loads[2:] + pair_loads + [out_load, up_load, down_load]:
-        copy.start()
 
     lane = lax.broadcasted_iota(jnp.int32, (1, width), 1)
     lane_head = sum((lane >= h * PAIR).astype(jnp.int32) for h in range(1, heads))
@@ -213,6 +210,8 @@
     value_mask = (lane_head == head_row) & is_value
     token_lane = lax.broadcasted_iota(jnp.int32, (1, tokens), 1)
 
+    for copy in cache_loads:
+        copy.wait()
     owners, limits, scores, peaks = [], [], [], []
     for b in range(blocks):
         owner = owner_ref[0, b]
@@ -220,8 +219,6 @@
         limit = jnp.where(
             owner < requests, length_ref[clipped] - index_ref[0, b] * tokens, 0
         )
-        if b in (0, middle):
-            cache_loads[b // middle].wait()
         q_row = q_rows[pl.ds(clipped, 1), :]
         block_query = jnp.where(key_mask, q_row, 0.0).astype(BF16)
         score = dot_last(block_query, cache[b])
@@ -230,6 +227,11 @@
         limits.append(limit)
         scores.append(score)
         peaks.append(jnp.max(score, axis=1, keepdims=True))
+
+    def values_only(wide):
+        return jnp.concatenate(
+            [wide[:, h * PAIR + HD : (h + 1) * PAIR] for h in range(heads)], axis=1
+        )
 
     slot_row = lax.broadcasted_iota(jnp.int32, (requests, 1), 0)
     sums = jnp.zeros((requests, width), F32)
@@ -258,7 +260,7 @@
             mine, jnp.where(small_lane < 8, stat_row, stats + stat_row), stats
         )
     stat_send[...] = stats.reshape(kvs, rows, 128)
-    sums_send[...] = sums.reshape(kvs, rows, width).astype(BF16)
+    sums_send[...] = values_only(sums).reshape(kvs, rows, heads * HD).astype(BF16)
 
     partial_sends = []
     for step in range(1, sources):
@@ -290,7 +292,7 @@
     for h in range(heads):
         score = jnp.sum(jnp.where(lane_head == h, self_products, 0.0), axis=1, keepdims=True)
         self_score = jnp.where(small_lane == h, score, self_score)
-    fresh_values = jnp.where(is_value, fresh, 0.0)
+    fresh_values = values_only(fresh)
 
     row_number = lax.broadcasted_iota(jnp.int32, (rows, 1), 0)
     target = jnp.zeros((rows, 1), jnp.int32)
@@ -316,10 +318,12 @@
                 device_id_type=MESH,
             ).wait_recv()
 
+    value_lane = lax.broadcasted_iota(jnp.int32, (1, heads * HD), 1)
+
     def over_lanes(values):
-        wide = jnp.broadcast_to(values[:, heads - 1 : heads], (rows, width))
+        wide = jnp.broadcast_to(values[:, heads - 1 : heads], (rows, heads * HD))
         for h in reversed(range(heads - 1)):
-            wide = jnp.where(lane < (h + 1) * PAIR, values[:, h : h + 1], wide)
+            wide = jnp.where(value_lane < (h + 1) * HD, values[:, h : h + 1], wide)
         return wide
 
     top = self_score
@@ -338,9 +342,7 @@
     attended = over_lanes(self_weight.astype(BF16).astype(F32) * share) * fresh_values
     for s in range(sources):
         attended = attended + over_lanes(factors[s] * share) * sums_recv[s].astype(F32)
-    attended = jnp.concatenate(
-        [attended[:, h * PAIR + HD : (h + 1) * PAIR] for h in range(heads)], axis=1
-    ).astype(BF16)
+    attended = attended.astype(BF16)
 
     def summed_over_tp(part, buffer, send_sem, recv_sem):
         buffer[tp] = part.astype(BF16)
@@ -442,14 +444,14 @@
             pltpu.VMEM((kvs, rows, width), BF16),
             pltpu.VMEM((requests, width), F32),
             pltpu.VMEM((kvs, rows, 128), F32),
-            pltpu.VMEM((kvs, rows, width), BF16),
+            pltpu.VMEM((kvs, rows, heads * HD), BF16),
             pltpu.VMEM((sources, rows, 128), F32),
-            pltpu.VMEM((sources, rows, width), BF16),
+            pltpu.VMEM((sources, rows, heads * HD), BF16),
             pltpu.VMEM((tps, rows, model), BF16),
             pltpu.VMEM((tps, rows, model), BF16),
             dma((8,)),
             dma((2 * heads + 3,)),
-            dma((2,)),
+            dma((blocks,)),
             dma((kvs,)),
             dma((kvs,)),
             dma((sources,)),

time: 27.4 us -> 27.1 us (0.989)
  Pallas kernels: 25.4 us -> 25.1 us
    pallas_call x1, Pallas kernels: 25.4 us -> 25.1 us  [body(): pl.pallas_call(functools.partial(kernel, sizes), out_shape=(pltpu.VMEM((1...]
where the time goes in v5:
time: 27.1 us; the launch traced here: 26.9 us
  Pallas kernels  25.1 us (93%)
  local copies, waits for them, and re-layouts  1.23 us (5%)
  between operations  0.64 us (2%)
    pallas_call x1, Pallas kernels, body(): pl.pallas_call(functools.partial(kernel, sizes), out_shape=(pltpu.VMEM((1...  25.1 us
    unnamed x2, local copies, waits for them, and re-layouts  1.23 us

profile of v5, /device:TPU:0, one launch (start us, length us, event | category | flops | bytes accessed | tf_op | source)
XLA Modules:
  0.0 26.9 jit_solution(8358740669076106937)
XLA Ops:
  0.6 25.1 %decode_layer.1 = (f32[1,8,1280]{2,1,0:T(8,128)S(1)}, f32[1,8,640]{2,1,0:T(8,128)S(1)}) custom-call(bf16[8,1280]{1,0:T(8,128)(2,1)} %state_hbm.1, f32[1280]{0:T(1024)} %attn_gain_hbm.1, f32[1280]{0:T(1024)} %mlp_gain_hbm.1, s32[32]{0:T(128)} %home_hbm.1, s32[32]{0:T(128)} %moving_hbm.1, s32[32]{0:T(128)} %length_hbm.1, s32[1,11]{1,0:T(1,128)} %owner_hbm.1, ...), custom_call_target="tpu_custom_call" | custom-call | tf_op jit(solution)/shard_map/decode_layer/pallas_call | solution.py:421
  25.7 0.6 %copy.17 = f32[1,8,1280]{2,1,0:T(8,128)} copy(f32[1,8,1280]{2,1,0:T(8,128)S(1)} %get-tuple-element.2) | data formatting | bytes 81920
  26.3 0.6 %copy.18 = f32[1,8,640]{2,1,0:T(8,128)} copy(f32[1,8,640]{2,1,0:T(8,128)S(1)} %get-tuple-element.3) | data formatting | bytes 40960

commit v6 on v5

--- a/solution.py
+++ b/solution.py
@@ -212,7 +212,7 @@
 
     for copy in cache_loads:
         copy.wait()
-    owners, limits, scores, peaks = [], [], [], []
+    owners, peaks, totals, accs = [], [], [], []
     for b in range(blocks):
         owner = owner_ref[0, b]
         clipped = jnp.minimum(owner, requests - 1)
@@ -222,11 +222,14 @@
         q_row = q_rows[pl.ds(clipped, 1), :]
         block_query = jnp.where(key_mask, q_row, 0.0).astype(BF16)
         score = dot_last(block_query, cache[b])
-        score = jnp.where(token_lane < limit, score, very_low)
+        usable = token_lane < limit
+        score = jnp.where(usable, score, very_low)
+        peak = jnp.max(score, axis=1, keepdims=True)
+        weight = jnp.where(usable, jnp.exp(score - peak), 0.0)
         owners.append(owner)
-        limits.append(limit)
-        scores.append(score)
-        peaks.append(jnp.max(score, axis=1, keepdims=True))
+        peaks.append(peak)
+        totals.append(jnp.sum(weight, axis=1, keepdims=True))
+        accs.append(dot_plain(weight.astype(BF16), cache[b]))
 
     def values_only(wide):
         return jnp.concatenate(
@@ -243,10 +246,9 @@
                 shift = jnp.where(
                     owners[other] == owners[b], jnp.maximum(shift, peaks[other]), shift
                 )
-        weight = jnp.where(token_lane < limits[b], jnp.exp(scores[b] - shift), 0.0)
-        total = jnp.sum(weight, axis=1, keepdims=True)
-        acc = dot_plain(weight.astype(BF16), cache[b])
-        acc_row = jnp.sum(jnp.where(value_mask, acc, 0.0), axis=0, keepdims=True)
+        scale = jnp.exp(peaks[b] - shift)
+        total = totals[b] * scale
+        acc_row = jnp.sum(jnp.where(value_mask, accs[b] * scale, 0.0), axis=0, keepdims=True)
         stat_row = jnp.sum(
             jnp.where(
                 small_lane == head_row, shift, jnp.where(small_lane == head_row + 8, total, 0.0)

time: 27.1 us -> 28.8 us (1.063)
  Pallas kernels: 25.1 us -> 26.8 us
    pallas_call x1, Pallas kernels: 25.1 us -> 26.8 us  [body(): pl.pallas_call(functools.partial(kernel, sizes), out_shape=(pltpu.VMEM((1...]
where the time goes in v6:
time: 28.8 us; the launch traced here: 28.7 us
  Pallas kernels  26.8 us (93%)
  local copies, waits for them, and re-layouts  1.23 us (4%)
  between operations  0.64 us (2%)
    pallas_call x1, Pallas kernels, body(): pl.pallas_call(functools.partial(kernel, sizes), out_shape=(pltpu.VMEM((1...  26.8 us
    unnamed x2, local copies, waits for them, and re-layouts  1.23 us

profile of v6, /device:TPU:0, one launch (start us, length us, event | category | flops | bytes accessed | tf_op | source)
XLA Modules:
  0.0 28.7 jit_solution(11873028925853942384)
XLA Ops:
  0.6 26.8 %decode_layer.1 = (f32[1,8,1280]{2,1,0:T(8,128)S(1)}, f32[1,8,640]{2,1,0:T(8,128)S(1)}) custom-call(bf16[8,1280]{1,0:T(8,128)(2,1)} %state_hbm.1, f32[1280]{0:T(1024)} %attn_gain_hbm.1, f32[1280]{0:T(1024)} %mlp_gain_hbm.1, s32[32]{0:T(128)} %home_hbm.1, s32[32]{0:T(128)} %moving_hbm.1, s32[32]{0:T(128)} %length_hbm.1, s32[1,11]{1,0:T(1,128)} %owner_hbm.1, ...), custom_call_target="tpu_custom_call" | custom-call | tf_op jit(solution)/shard_map/decode_layer/pallas_call | solution.py:423
  27.5 0.6 %copy.17 = f32[1,8,1280]{2,1,0:T(8,128)} copy(f32[1,8,1280]{2,1,0:T(8,128)S(1)} %get-tuple-element.2) | data formatting | bytes 81920
  28.1 0.6 %copy.18 = f32[1,8,640]{2,1,0:T(8,128)} copy(f32[1,8,640]{2,1,0:T(8,128)S(1)} %get-tuple-element.3) | data formatting | bytes 40960
